TPU v7x, 32 devices: a whole 2x2x4 slice. The times are simulated.
32 devices in a mesh: pair: 2 (over y), rep: 4 (over x, core), blk: 4 (over z).
Axes of the slice: x: 2, y: 2, z: 4, core: 2. Of those that a mesh axis runs over, the one named last changes fastest.
Arguments:
- src_spectra: bfloat16 [64, 8192], P(None, ('pair', 'rep', 'blk')), parts along dimension 1, may hold values from -4 to 4
- tgt_spectra: bfloat16 [64, 8192], P(None, ('pair', 'blk')), parts along dimension 1, may hold values from -4 to 4
- log_src_weight: float32 [8192], P(('pair', 'rep', 'blk')), parts along dimension 0, may hold values from -2 to 2
- log_tgt_weight: float32 [8192], P(('pair', 'blk')), parts along dimension 0, may hold values from -2 to 2
- src_potential: float32 [8192], P(('pair', 'rep', 'blk')), parts along dimension 0, may hold values from -4 to 250
- tgt_potential: float32 [8192], P(('pair', 'blk')), parts along dimension 0, may hold values from -4 to 250
Outputs:
- src_updated: float32 [8192], P(('pair', 'rep', 'blk')), parts along dimension 0
- tgt_updated: float32 [8192], P(('pair', 'blk')), parts along dimension 0
There are 2 independent parts, one for each index of `pair`. A program takes and returns all parts, laid end to end along the dimension named above; each array names one. Nothing has to cross between parts.
All inputs are finite; a program needn't handle non-finite values.
Results may differ from a plain program's by a relative error of at most 0.0003.
Values may be sent and summed in bfloat16 or wider, within the bound.
A program may use at most 128 MiB of HBM per device.

v0:
```python
import jax
import jax.numpy as jnp
from jax import lax
from jax.sharding import PartitionSpec as P


def passed_along(value, axis, steps):
    count = lax.axis_size(axis)
    pairs = [(source, (source + steps) % count) for source in range(count)]
    return lax.ppermute(value, axis, pairs)


def merged(value, axis, join):
    pieces = jax.tree.map(lambda part: lax.all_gather(part, axis), value)
    head = jax.tree.map(lambda part: part[0], pieces)
    tail = jax.tree.map(lambda part: part[1:], pieces)
    so_far, _ = lax.scan(lambda so_far, share: (join(so_far, share), None), head, tail)
    return so_far


def peaks_join(earlier, later):
    joined = jnp.maximum(earlier[0], later[0])
    return (
        joined,
        earlier[1] * jnp.exp(earlier[0] - joined) + later[1] * jnp.exp(later[0] - joined),
    )


def tile_scores(src_spectra, src_square, src_bias, tgt_bias, spectra_piece, offset):
    width = spectra_piece.shape[1]
    piece_float = spectra_piece.astype(jnp.float32)
    tgt_square = 0.5 * jnp.sum(piece_float * piece_float, axis=0)
    products = lax.dot_general(
        src_spectra, spectra_piece, (((0,), (0,)), ((), ())), preferred_element_type=jnp.float32
    )
    cost_tile = src_square[:, None] + tgt_square[None, :] - products
    bias_piece = lax.dynamic_slice_in_dim(tgt_bias, offset, width, 0)
    return (bias_piece[None, :] - cost_tile, src_bias[:, None] - cost_tile)


def row_update(row_peak, row_totals, row_scores):
    joined = jnp.maximum(row_peak, jnp.max(row_scores, axis=1))
    fresh = jnp.sum(jnp.exp(row_scores - joined[:, None]), axis=1)
    return (joined, row_totals * jnp.exp(row_peak - joined) + fresh)


def column_part(col_scores):
    block_peak = jnp.max(col_scores, axis=0)
    return (block_peak, jnp.sum(jnp.exp(col_scores - block_peak[None, :]), axis=0))


def on_device(
    src_spectra, tgt_spectra, log_src_weight, log_tgt_weight, src_potential, tgt_potential
):
    src_float = src_spectra.astype(jnp.float32)
    src_square = 0.5 * jnp.sum(src_float * src_float, axis=0)
    src_bias = log_src_weight + src_potential
    tgt_bias = lax.all_gather(log_tgt_weight + tgt_potential, "blk", axis=0, tiled=True)
    own_width = tgt_spectra.shape[1]
    everything = tgt_bias.shape[0]
    rows_here = src_spectra.shape[1]
    start_peak = jnp.full((rows_here,), -jnp.inf, jnp.float32)
    start_totals = jnp.zeros((rows_here,), jnp.float32)
    shards = everything // own_width
    home = lax.axis_index("blk")

    def turn(turn_index, carry):
        row_peak, row_totals, spectra_piece, carried_peak, carried_totals = carry
        offset = (home - turn_index) % shards * own_width
        row_scores, col_scores = tile_scores(
            src_spectra, src_square, src_bias, tgt_bias, spectra_piece, offset
        )
        row_peak, row_totals = row_update(row_peak, row_totals, row_scores)
        carried_peak, carried_totals = peaks_join(
            (carried_peak, carried_totals), column_part(col_scores)
        )
        spectra_piece = passed_along(spectra_piece, "blk", 1)
        carried_peak, carried_totals = passed_along((carried_peak, carried_totals), "blk", 1)
        return (row_peak, row_totals, spectra_piece, carried_peak, carried_totals)

    carry = (
        start_peak,
        start_totals,
        tgt_spectra,
        jnp.full((own_width,), -jnp.inf, jnp.float32),
        jnp.zeros((own_width,), jnp.float32),
    )
    row_peak, row_totals, returned, carried_peak, carried_totals = lax.fori_loop(
        0, shards, turn, carry
    )
    mine_peak, mine_totals = merged((carried_peak, carried_totals), "rep", peaks_join)
    tgt_new = -(mine_peak + jnp.log(mine_totals))
    src_new = -(row_peak + jnp.log(row_totals))
    return (0.5 * (src_potential + src_new), 0.5 * (tgt_potential + tgt_new))


def solution(mesh):
    placed = (
        P(None, ("pair", "rep", "blk")),
        P(None, ("pair", "blk")),
        P(("pair", "rep", "blk")),
        P(("pair", "blk")),
        P(("pair", "rep", "blk")),
        P(("pair", "blk")),
    )
    return jax.shard_map(
        on_device,
        mesh=mesh,
        in_specs=placed,
        out_specs=(P(("pair", "rep", "blk")), P(("pair", "blk"))),
        check_vma=False,
    )
```

profile of v0, /device:TPU:0, one launch (start us, length us, event | category | flops | bytes accessed | tf_op | source)
XLA Modules:
  0.0 62.1 jit_solution(9020351512151376552)
XLA Ops:
  0.6 0.0 copy-start
  0.7 0.7 %copy-done.3 = f32[1024]{0:T(1024)S(1)} copy-done((f32[1024]{0:T(1024)S(1)}, f32[1024]{0:T(1024)}, u32[]{:S(2)}) %copy-start.3) | copy-done | bytes 4120
  1.4 0.0 copy-done.4
  1.4 14.8 %all_gather.15 = f32[4096]{0:T(1024)S(1)} all-gather(f32[1024]{0:T(1024)S(1)} %add.130), channel_id=1, replica_groups=mesh['pair'=2,'rep'=4,'blk'=4] {'blk'}, dimensions={0}, use_global_device_ids=true | all-gather | bytes 20480 | tf_op jit(solution)/shard_map/all_gather | solution.py:58
  16.2 0.0 copy-start.6
  16.2 0.0 copy-start.5
  16.2 0.7 %copy-done.6 = f32[256]{0:T(256)S(1)} copy-done((f32[256]{0:T(256)S(1)}, f32[256]{0:T(256)}, u32[]{:S(2)}) %copy-start.6) | copy-done | bytes 1048
  16.9 0.0 copy-done.5
  16.9 32.8 %while.37 = (s32[]{:T(128)}, f32[256]{0:T(256)S(1)}, f32[256]{0:T(256)S(1)}, bf16[64,1024]{1,0:T(8,128)(2,1)S(1)}, f32[1024]{0:T(1024)S(1)}, /*index=5*/f32[1024...) while((s32[]{:T(128)}, f32[256]{0:T(256)S(1)}, ...), condition=%wide.region_7.8_spmd.clone, body=%wide.region_1.7_spmd.clone.sunk | while | flops 36902160 | bytes 3297739 | solution.py:88
  17.0 1.6 %collective-permute-start = (bf16[64,1024]{1,0:T(8,128)(2,1)S(1)}, bf16[64,1024]{1,0:T(8,128)(2,1)S(1)}, u32[]{:S(2)}, u32[]{:S(2)}) collective-permute-start(bf16[64,1024]{1,0:T(8,128)(2,1)S(1)} %copy.17), channel_id=1, source_target_pairs={{0,1},{1,2},{2,3},{3,0},{4,5},{5,6},{6,7},{7,4},{8,9},{9,10},{10,1... | collective-permute-start | bytes 393224 | tf_op jit(solution)/shard_map/while/body/eval_jaxpr/ppermute | solution.py:10
  18.7 0.5 subtract_reduce_fusion.3
  19.2 0.4 exponential_reduce_fusion.3
  19.6 0.1 collective-permute-start.1
  19.7 2.9 %collective-permute-start.2 = (f32[1024]{0:T(1024)S(1)}, f32[1024]{0:T(1024)S(1)}, u32[]{:S(2)}, u32[]{:S(2)}) collective-permute-start(f32[1024]{0:T(1024)S(1)} %get-tuple-element.502), channel_id=1, source_target_pairs={{0,1},{1,2},{2,3},{3,0},{4,5},{5,6},{6,7},{7,4},{8,9},{9,10},{10,1... | collective-permute-start | bytes 12296 | tf_op jit(solution)/shard_map/while/body/eval_jaxpr/ppermute | solution.py:10
  22.7 2.4 %collective-permute-done.1 = f32[1024]{0:T(1024)S(1)} collective-permute-done((f32[1024]{0:T(1024)S(1)}, f32[1024]{0:T(1024)S(1)}, u32[]{:S(2)}, u32[]{:S(2)}) %collective-permute-start.1) | collective-permute-done | bytes 4128 | tf_op jit(solution)/shard_map/while/body/eval_jaxpr/ppermute | solution.py:10
  25.1 0.1 collective-permute-done.2
  25.2 0.0 collective-permute-done
  25.2 1.1 %collective-permute-start = (bf16[64,1024]{1,0:T(8,128)(2,1)S(1)}, bf16[64,1024]{1,0:T(8,128)(2,1)S(1)}, u32[]{:S(2)}, u32[]{:S(2)}) collective-permute-start(bf16[64,1024]{1,0:T(8,128)(2,1)S(1)} %copy.17), channel_id=1, source_target_pairs={{0,1},{1,2},{2,3},{3,0},{4,5},{5,6},{6,7},{7,4},{8,9},{9,10},{10,1... | collective-permute-start | bytes 393224 | tf_op jit(solution)/shard_map/while/body/eval_jaxpr/ppermute | solution.py:10
  26.4 0.5 subtract_reduce_fusion.3
  26.9 0.4 exponential_reduce_fusion.3
  27.4 0.5 collective-permute-start.1
  27.9 1.6 %collective-permute-start.2 = (f32[1024]{0:T(1024)S(1)}, f32[1024]{0:T(1024)S(1)}, u32[]{:S(2)}, u32[]{:S(2)}) collective-permute-start(f32[1024]{0:T(1024)S(1)} %get-tuple-element.502), channel_id=1, source_target_pairs={{0,1},{1,2},{2,3},{3,0},{4,5},{5,6},{6,7},{7,4},{8,9},{9,10},{10,1... | collective-permute-start | bytes 12296 | tf_op jit(solution)/shard_map/while/body/eval_jaxpr/ppermute | solution.py:10
  29.5 3.5 %collective-permute-done.1 = f32[1024]{0:T(1024)S(1)} collective-permute-done((f32[1024]{0:T(1024)S(1)}, f32[1024]{0:T(1024)S(1)}, u32[]{:S(2)}, u32[]{:S(2)}) %collective-permute-start.1) | collective-permute-done | bytes 4128 | tf_op jit(solution)/shard_map/while/body/eval_jaxpr/ppermute | solution.py:10
  32.9 0.4 collective-permute-done.2
  33.4 0.0 collective-permute-done
  33.4 0.1 collective-permute-start
  33.6 0.5 subtract_reduce_fusion.3
  34.1 0.4 exponential_reduce_fusion.3
  34.5 1.6 %collective-permute-start.1 = (f32[1024]{0:T(1024)S(1)}, f32[1024]{0:T(1024)S(1)}, u32[]{:S(2)}, u32[]{:S(2)}) collective-permute-start(f32[1024]{0:T(1024)S(1)} %get-tuple-element.501), channel_id=1, source_target_pairs={{0,1},{1,2},{2,3},{3,0},{4,5},{5,6},{6,7},{7,4},{8,9},{9,10},{10,1... | collective-permute-start | bytes 12296 | tf_op jit(solution)/shard_map/while/body/eval_jaxpr/ppermute | solution.py:10
  36.1 1.0 %collective-permute-start.2 = (f32[1024]{0:T(1024)S(1)}, f32[1024]{0:T(1024)S(1)}, u32[]{:S(2)}, u32[]{:S(2)}) collective-permute-start(f32[1024]{0:T(1024)S(1)} %get-tuple-element.502), channel_id=1, source_target_pairs={{0,1},{1,2},{2,3},{3,0},{4,5},{5,6},{6,7},{7,4},{8,9},{9,10},{10,1... | collective-permute-start | bytes 12296 | tf_op jit(solution)/shard_map/while/body/eval_jaxpr/ppermute | solution.py:10
  37.2 3.8 %collective-permute-done.1 = f32[1024]{0:T(1024)S(1)} collective-permute-done((f32[1024]{0:T(1024)S(1)}, f32[1024]{0:T(1024)S(1)}, u32[]{:S(2)}, u32[]{:S(2)}) %collective-permute-start.1) | collective-permute-done | bytes 4128 | tf_op jit(solution)/shard_map/while/body/eval_jaxpr/ppermute | solution.py:10
  41.0 0.5 collective-permute-done.2
  41.5 0.0 collective-permute-done
  41.5 0.1 collective-permute-start
  41.7 0.5 subtract_reduce_fusion.3
  42.2 0.4 exponential_reduce_fusion.3
  42.7 1.6 %collective-permute-start.1 = (f32[1024]{0:T(1024)S(1)}, f32[1024]{0:T(1024)S(1)}, u32[]{:S(2)}, u32[]{:S(2)}) collective-permute-start(f32[1024]{0:T(1024)S(1)} %get-tuple-element.501), channel_id=1, source_target_pairs={{0,1},{1,2},{2,3},{3,0},{4,5},{5,6},{6,7},{7,4},{8,9},{9,10},{10,1... | collective-permute-start | bytes 12296 | tf_op jit(solution)/shard_map/while/body/eval_jaxpr/ppermute | solution.py:10
  44.3 0.1 collective-permute-start.2
  44.4 4.0 %collective-permute-done.1 = f32[1024]{0:T(1024)S(1)} collective-permute-done((f32[1024]{0:T(1024)S(1)}, f32[1024]{0:T(1024)S(1)}, u32[]{:S(2)}, u32[]{:S(2)}) %collective-permute-start.1) | collective-permute-done | bytes 4128 | tf_op jit(solution)/shard_map/while/body/eval_jaxpr/ppermute | solution.py:10
  48.4 1.3 %collective-permute-done.2 = f32[1024]{0:T(1024)S(1)} collective-permute-done((f32[1024]{0:T(1024)S(1)}, f32[1024]{0:T(1024)S(1)}, u32[]{:S(2)}, u32[]{:S(2)}) %collective-permute-start.2) | collective-permute-done | bytes 4128 | tf_op jit(solution)/shard_map/while/body/eval_jaxpr/ppermute | solution.py:10
  49.7 0.0 collective-permute-done
  49.7 5.2 %all-gather = f32[4096]{0:T(1024)S(1)} all-gather(f32[1024]{0:T(1024)S(1)} %get-tuple-element.300), channel_id=2, replica_groups=mesh['pair'=2,'rep'=4,'blk'=4] {'rep'}, dimensions={0}, use_global_device_ids=true | all-gather | bytes 20480 | tf_op jit(solution)/shard_map/all_gather | solution.py:14
  54.9 5.2 %all-gather.1 = f32[4096]{0:T(1024)S(1)} all-gather(f32[1024]{0:T(1024)S(1)} %get-tuple-element.301), channel_id=3, replica_groups=mesh['pair'=2,'rep'=4,'blk'=4] {'rep'}, dimensions={0}, use_global_device_ids=true | all-gather | bytes 20480 | tf_op jit(solution)/shard_map/all_gather | solution.py:14
  60.1 0.0 slice-start
  60.1 0.7 %slice-done = f32[1024]{0:T(1024)S(1)} async-done(((f32[4096]{0:T(1024)}), f32[1024]{0:T(1024)S(1)}, s32[]{:S(2)}) %slice-start) | async-done | bytes 4120 | tf_op jit(solution)/shard_map/slice | solution.py:15
  60.8 0.1 while.36
  60.9 0.6 add_multiply_fusion
  61.5 0.6 add_multiply_fusion.1
  (58 shorter events, 0.5 us)
Async XLA Ops:
  0.6 16.3 %copy-start = (bf16[64,1024]{1,0:T(8,128)(2,1)S(1)}, bf16[64,1024]{1,0:T(8,128)(2,1)}, u32[]{:S(2)}) copy-start(bf16[64,1024]{1,0:T(8,128)(2,1)} %param.11) | copy-start | bytes 393220
  0.6 0.7 %copy-start.3 = (f32[1024]{0:T(1024)S(1)}, f32[1024]{0:T(1024)}, u32[]{:S(2)}) copy-start(f32[1024]{0:T(1024)} %param.15) | copy-start | bytes 12292
  0.7 0.7 %copy-start.4 = (f32[1024]{0:T(1024)S(1)}, f32[1024]{0:T(1024)}, u32[]{:S(2)}) copy-start(f32[1024]{0:T(1024)} %param.13) | copy-start | bytes 12292
  0.7 15.5 %copy-start.2 = (bf16[64,256]{1,0:T(8,128)(2,1)S(1)}, bf16[64,256]{1,0:T(8,128)(2,1)}, u32[]{:S(2)}) copy-start(bf16[64,256]{1,0:T(8,128)(2,1)} %param.10) | copy-start | bytes 98308
  16.2 0.7 %copy-start.6 = (f32[256]{0:T(256)S(1)}, f32[256]{0:T(256)}, u32[]{:S(2)}) copy-start(f32[256]{0:T(256)} %param.12) | copy-start | bytes 3076
  16.2 0.7 %copy-start.5 = (f32[256]{0:T(256)S(1)}, f32[256]{0:T(256)}, u32[]{:S(2)}) copy-start(f32[256]{0:T(256)} %param.14) | copy-start | bytes 3076
  17.0 8.2 %collective-permute-start = (bf16[64,1024]{1,0:T(8,128)(2,1)S(1)}, bf16[64,1024]{1,0:T(8,128)(2,1)S(1)}, u32[]{:S(2)}, u32[]{:S(2)}) collective-permute-start(bf16[64,1024]{1,0:T(8,128)(2,1)S(1)} %copy.17), channel_id=1, source_target_pairs={{0,1},{1,2},{2,3},{3,0},{4,5},{5,6},{6,7},{7,4},{8,9},{9,10},{10,1... | collective-permute-start | bytes 393224 | tf_op jit(solution)/shard_map/while/body/eval_jaxpr/ppermute | solution.py:10
  19.6 5.5 %collective-permute-start.1 = (f32[1024]{0:T(1024)S(1)}, f32[1024]{0:T(1024)S(1)}, u32[]{:S(2)}, u32[]{:S(2)}) collective-permute-start(f32[1024]{0:T(1024)S(1)} %get-tuple-element.501), channel_id=1, source_target_pairs={{0,1},{1,2},{2,3},{3,0},{4,5},{5,6},{6,7},{7,4},{8,9},{9,10},{10,1... | collective-permute-start | bytes 12296 | tf_op jit(solution)/shard_map/while/body/eval_jaxpr/ppermute | solution.py:10
  19.7 5.5 %collective-permute-start.2 = (f32[1024]{0:T(1024)S(1)}, f32[1024]{0:T(1024)S(1)}, u32[]{:S(2)}, u32[]{:S(2)}) collective-permute-start(f32[1024]{0:T(1024)S(1)} %get-tuple-element.502), channel_id=1, source_target_pairs={{0,1},{1,2},{2,3},{3,0},{4,5},{5,6},{6,7},{7,4},{8,9},{9,10},{10,1... | collective-permute-start | bytes 12296 | tf_op jit(solution)/shard_map/while/body/eval_jaxpr/ppermute | solution.py:10
  25.2 8.2 %collective-permute-start = (bf16[64,1024]{1,0:T(8,128)(2,1)S(1)}, bf16[64,1024]{1,0:T(8,128)(2,1)S(1)}, u32[]{:S(2)}, u32[]{:S(2)}) collective-permute-start(bf16[64,1024]{1,0:T(8,128)(2,1)S(1)} %copy.17), channel_id=1, source_target_pairs={{0,1},{1,2},{2,3},{3,0},{4,5},{5,6},{6,7},{7,4},{8,9},{9,10},{10,1... | collective-permute-start | bytes 393224 | tf_op jit(solution)/shard_map/while/body/eval_jaxpr/ppermute | solution.py:10
  27.4 5.6 %collective-permute-start.1 = (f32[1024]{0:T(1024)S(1)}, f32[1024]{0:T(1024)S(1)}, u32[]{:S(2)}, u32[]{:S(2)}) collective-permute-start(f32[1024]{0:T(1024)S(1)} %get-tuple-element.501), channel_id=1, source_target_pairs={{0,1},{1,2},{2,3},{3,0},{4,5},{5,6},{6,7},{7,4},{8,9},{9,10},{10,1... | collective-permute-start | bytes 12296 | tf_op jit(solution)/shard_map/while/body/eval_jaxpr/ppermute | solution.py:10
  27.9 5.5 %collective-permute-start.2 = (f32[1024]{0:T(1024)S(1)}, f32[1024]{0:T(1024)S(1)}, u32[]{:S(2)}, u32[]{:S(2)}) collective-permute-start(f32[1024]{0:T(1024)S(1)} %get-tuple-element.502), channel_id=1, source_target_pairs={{0,1},{1,2},{2,3},{3,0},{4,5},{5,6},{6,7},{7,4},{8,9},{9,10},{10,1... | collective-permute-start | bytes 12296 | tf_op jit(solution)/shard_map/while/body/eval_jaxpr/ppermute | solution.py:10
  33.4 8.1 %collective-permute-start = (bf16[64,1024]{1,0:T(8,128)(2,1)S(1)}, bf16[64,1024]{1,0:T(8,128)(2,1)S(1)}, u32[]{:S(2)}, u32[]{:S(2)}) collective-permute-start(bf16[64,1024]{1,0:T(8,128)(2,1)S(1)} %copy.17), channel_id=1, source_target_pairs={{0,1},{1,2},{2,3},{3,0},{4,5},{5,6},{6,7},{7,4},{8,9},{9,10},{10,1... | collective-permute-start | bytes 393224 | tf_op jit(solution)/shard_map/while/body/eval_jaxpr/ppermute | solution.py:10
  34.5 6.5 %collective-permute-start.1 = (f32[1024]{0:T(1024)S(1)}, f32[1024]{0:T(1024)S(1)}, u32[]{:S(2)}, u32[]{:S(2)}) collective-permute-start(f32[1024]{0:T(1024)S(1)} %get-tuple-element.501), channel_id=1, source_target_pairs={{0,1},{1,2},{2,3},{3,0},{4,5},{5,6},{6,7},{7,4},{8,9},{9,10},{10,1... | collective-permute-start | bytes 12296 | tf_op jit(solution)/shard_map/while/body/eval_jaxpr/ppermute | solution.py:10
  36.1 5.4 %collective-permute-start.2 = (f32[1024]{0:T(1024)S(1)}, f32[1024]{0:T(1024)S(1)}, u32[]{:S(2)}, u32[]{:S(2)}) collective-permute-start(f32[1024]{0:T(1024)S(1)} %get-tuple-element.502), channel_id=1, source_target_pairs={{0,1},{1,2},{2,3},{3,0},{4,5},{5,6},{6,7},{7,4},{8,9},{9,10},{10,1... | collective-permute-start | bytes 12296 | tf_op jit(solution)/shard_map/while/body/eval_jaxpr/ppermute | solution.py:10
  41.5 8.2 %collective-permute-start = (bf16[64,1024]{1,0:T(8,128)(2,1)S(1)}, bf16[64,1024]{1,0:T(8,128)(2,1)S(1)}, u32[]{:S(2)}, u32[]{:S(2)}) collective-permute-start(bf16[64,1024]{1,0:T(8,128)(2,1)S(1)} %copy.17), channel_id=1, source_target_pairs={{0,1},{1,2},{2,3},{3,0},{4,5},{5,6},{6,7},{7,4},{8,9},{9,10},{10,1... | collective-permute-start | bytes 393224 | tf_op jit(solution)/shard_map/while/body/eval_jaxpr/ppermute | solution.py:10
  42.7 5.7 %collective-permute-start.1 = (f32[1024]{0:T(1024)S(1)}, f32[1024]{0:T(1024)S(1)}, u32[]{:S(2)}, u32[]{:S(2)}) collective-permute-start(f32[1024]{0:T(1024)S(1)} %get-tuple-element.501), channel_id=1, source_target_pairs={{0,1},{1,2},{2,3},{3,0},{4,5},{5,6},{6,7},{7,4},{8,9},{9,10},{10,1... | collective-permute-start | bytes 12296 | tf_op jit(solution)/shard_map/while/body/eval_jaxpr/ppermute | solution.py:10
  44.3 5.4 %collective-permute-start.2 = (f32[1024]{0:T(1024)S(1)}, f32[1024]{0:T(1024)S(1)}, u32[]{:S(2)}, u32[]{:S(2)}) collective-permute-start(f32[1024]{0:T(1024)S(1)} %get-tuple-element.502), channel_id=1, source_target_pairs={{0,1},{1,2},{2,3},{3,0},{4,5},{5,6},{6,7},{7,4},{8,9},{9,10},{10,1... | collective-permute-start | bytes 12296 | tf_op jit(solution)/shard_map/while/body/eval_jaxpr/ppermute | solution.py:10
  54.9 5.2 %copy-start.1 = (f32[4096]{0:T(1024)}, f32[4096]{0:T(1024)S(1)}, u32[]{:S(2)}) copy-start(f32[4096]{0:T(1024)S(1)} %all-gather) | copy-start | bytes 49156
  60.1 0.7 %slice-start = ((f32[4096]{0:T(1024)}), f32[1024]{0:T(1024)S(1)}, s32[]{:S(2)}) async-start(f32[4096]{0:T(1024)} %copy-done.1), calls=%async_computation | async-start | bytes 8192 | tf_op jit(solution)/shard_map/slice | solution.py:15
where the time goes:
time: 62.3 us; the launch traced here: 62.1 us
  blocking collectives  25.1 us (40%)
  waiting for transfers between devices  16.1 us (26%)
  starting transfers between devices  12.2 us (20%)
  other arithmetic  3.3 us (5%)
  local copies, waits for them, and re-layouts  2.21 us (4%)
  matrix products  1.93 us (3%)
  between operations  0.73 us (1%)
    ppermute x12, waiting for transfers between devices, passed_along(): return lax.ppermute(value, axis, pairs)  16.1 us
    all_gather x1, blocking collectives, on_device(): lax.all_gather(log_tgt_weight + tgt_potential, 'blk', axis=0, tiled=True)  14.8 us
    ppermute x12, starting transfers between devices, passed_along(): return lax.ppermute(value, axis, pairs)  12.2 us
    all_gather x2, blocking collectives, merged(): pieces = jax.tree.map(lambda part: lax.all_gather(part, axis), value)  10.4 us
    dot_general x4, matrix products, tile_scores(): lax.dot_general(src_spectra, spectra_piece, (((0,), (0,)), ((), ())), pre...  1.93 us
    reduce_sum x4, other arithmetic, column_part(): jnp.sum(jnp.exp(col_scores - block_peak[None, :]), axis=0)  1.74 us
    unnamed x14, local copies, waits for them, and re-layouts  1.4 us
  transfers between devices with their start and end apart: 12, of which 8 were waited for; matrix products, arithmetic and copies ran while one was open for 6% of the time, Pallas kernels for 0%

commit v1 on v0

v1 whole, which is shorter than its diff:
```python
import functools

import jax
import jax.numpy as jnp
from jax import lax
from jax.experimental import pallas as pl
from jax.experimental.pallas import tpu as pltpu
from jax.sharding import PartitionSpec as P

MESH = pl.DeviceIdType.MESH
SUBLANES = 8
EXTRA = 16
TILE = 256


def nearest(me, count, k):
    short = jnp.minimum(me, count - 1 - me)
    step = (k + 1) // 2
    both = me + jnp.where(k % 2 == 1, step, -step)
    both = jnp.where(me * 2 < count, both, 2 * me - both)
    far = jnp.where(me * 2 < count, k, count - 1 - k)
    return jnp.where(k <= 2 * short, both, far)


def in_three(value):
    high = value.astype(jnp.bfloat16).astype(jnp.float32)
    middle = (value - high).astype(jnp.bfloat16).astype(jnp.float32)
    return high, middle, value - high - middle


def bias_rows(value, first):
    high, middle, low = in_three(value)
    row = lax.broadcasted_iota(jnp.int32, (EXTRA, value.shape[1]), 0)
    out = jnp.where(row < 6, 1.0, 0.0)
    out = jnp.where(row == first, high, out)
    out = jnp.where(row == first + 1, middle, out)
    out = jnp.where(row == first + 2, low, out)
    return out.astype(jnp.bfloat16)


def half_square(block):
    wide = block.astype(jnp.float32)
    return 0.5 * jnp.sum(wide * wide, axis=0, keepdims=True)


def peak_and_sum(scores):
    rows, width = scores.shape
    grouped = scores.reshape(rows // SUBLANES, SUBLANES, width)
    peak = jnp.max(grouped, axis=0)
    return peak, jnp.sum(jnp.exp(grouped - peak[None]), axis=0)


def joined(earlier, later):
    peak = jnp.maximum(earlier[0], later[0])
    return peak, earlier[1] * jnp.exp(earlier[0] - peak) + later[1] * jnp.exp(later[0] - peak)


def folded(peak, total):
    top = jnp.max(peak, axis=0, keepdims=True)
    return top, jnp.sum(total * jnp.exp(peak - top), axis=0, keepdims=True)


def kernel(
    blocks, copies,
    src_hbm, tgt_hbm, lsw_hbm, ltw_hbm, sp_hbm, tp_hbm,
    src_out, tgt_out,
    slots, biases, tgt_v, lsw, ltw, sp, tp, tgt_flat, tgt_tall, row_mine, row_stats, col_peak, col_total,
    col_stats,
    load_sem, slot_send, slot_recv, bias_send, bias_recv, row_send, row_recv, col_send, col_recv,
):
    me = lax.axis_index("blk")
    rep = lax.axis_index("rep")
    bands, width = src_hbm.shape
    tgt_width = tgt_hbm.shape[1]

    barrier = pltpu.get_barrier_semaphore()
    for k in range(1, blocks):
        pl.semaphore_signal(
            barrier, inc=1, device_id={"blk": (me + k) % blocks}, device_id_type=MESH
        )
    for k in range(1, copies):
        pl.semaphore_signal(
            barrier, inc=1, device_id={"rep": (rep + k) % copies}, device_id_type=MESH
        )
    loads = [
        pltpu.make_async_copy(src_hbm, slots.at[me], load_sem.at[0]),
        pltpu.make_async_copy(lsw_hbm, lsw, load_sem.at[1]),
        pltpu.make_async_copy(sp_hbm, sp, load_sem.at[2]),
        pltpu.make_async_copy(tgt_hbm, tgt_v, load_sem.at[3]),
        pltpu.make_async_copy(ltw_hbm, ltw, load_sem.at[4]),
        pltpu.make_async_copy(tp_hbm, tp, load_sem.at[5]),
    ]
    for load in loads:
        load.start()
    pl.semaphore_wait(barrier, blocks + copies - 2)

    def slot_copy(place, peer):
        return pltpu.make_async_remote_copy(
            src_ref=src_hbm, dst_ref=slots.at[place],
            send_sem=slot_send.at[peer], recv_sem=slot_recv.at[place],
            device_id={"blk": peer}, device_id_type=MESH,
        )

    def bias_copy(place, peer):
        return pltpu.make_async_remote_copy(
            src_ref=biases.at[me], dst_ref=biases.at[place],
            send_sem=bias_send.at[peer], recv_sem=bias_recv.at[place],
            device_id={"blk": peer}, device_id_type=MESH,
        )

    def row_copy(place, peer):
        return pltpu.make_async_remote_copy(
            src_ref=row_mine.at[peer], dst_ref=row_stats.at[place],
            send_sem=row_send.at[peer], recv_sem=row_recv.at[place],
            device_id={"blk": peer}, device_id_type=MESH,
        )

    def col_copy(place, peer):
        return pltpu.make_async_remote_copy(
            src_ref=col_stats.at[rep], dst_ref=col_stats.at[place],
            send_sem=col_send.at[peer], recv_sem=col_recv.at[place],
            device_id={"rep": peer}, device_id_type=MESH,
        )

    for k in range(1, blocks):
        slot_copy(me, nearest(me, blocks, k)).start()
    for load in loads[:3]:
        load.wait()
    src_bias = lsw[...] + sp[...]
    biases[me] = src_bias - half_square(slots[me])
    for k in range(1, blocks):
        bias_copy(me, nearest(me, blocks, k)).start()
    for load in loads[3:]:
        load.wait()
    tgt_bias = ltw[...] + tp[...]
    tgt_flat[pl.ds(0, bands), :] = tgt_v[...]
    tgt_flat[pl.ds(bands, EXTRA), :] = bias_rows(tgt_bias - half_square(tgt_v[...]), 3)
    for at in range(0, tgt_width, TILE):
        tgt_tall[pl.ds(at, TILE), :] = tgt_flat[:, pl.ds(at, TILE)].T
    col_peak[...] = jnp.full_like(col_peak, -jnp.inf)
    col_total[...] = jnp.zeros_like(col_total)

    def turn(k, carry):
        place = nearest(me, blocks, k)

        @pl.when(k > 0)
        def _():
            slot_copy(place, place).wait_recv()
            bias_copy(place, place).wait_recv()

        src = jnp.concatenate([slots[place], bias_rows(biases[place], 0)], axis=0)
        src_tall = src.T
        row = None
        for at in range(0, tgt_width, TILE):
            across = jnp.dot(
                tgt_tall[pl.ds(at, TILE), :], src, preferred_element_type=jnp.float32
            )
            part = peak_and_sum(across)
            row = part if row is None else joined(row, part)
            down = jnp.dot(
                src_tall, tgt_flat[:, pl.ds(at, TILE)], preferred_element_type=jnp.float32
            )
            here = (slice(None), pl.ds(at, TILE))
            col_peak[here], col_total[here] = joined(
                (col_peak[here], col_total[here]), peak_and_sum(down)
            )
        top, total = folded(*row)
        stats = jnp.concatenate([top, total], axis=0)

        @pl.when(k > 0)
        def _():
            row_mine[place] = stats
            row_copy(me, place).start()

        @pl.when(k == 0)
        def _():
            row_stats[me] = stats

        return carry

    lax.fori_loop(0, blocks, turn, 0)
    top, total = folded(col_peak[...], col_total[...])
    col_stats[rep] = jnp.concatenate([top, total], axis=0)
    for k in range(1, copies):
        col_copy(rep, (rep + k) % copies).start()

    for k in range(1, blocks):
        place = nearest(me, blocks, k)
        row_copy(place, place).wait_recv()
    every = row_stats[...]
    top = jnp.max(every[:, 0, :], axis=0, keepdims=True)
    total = jnp.sum(every[:, 1, :] * jnp.exp(every[:, 0, :] - top), axis=0, keepdims=True)
    src_out[...] = 0.5 * (sp[...] + (src_bias - (top + jnp.log(total))))

    for k in range(1, copies):
        place = (rep + k) % copies
        col_copy(place, place).wait_recv()
    every = col_stats[...]
    top = jnp.max(every[:, 0, :], axis=0, keepdims=True)
    total = jnp.sum(every[:, 1, :] * jnp.exp(every[:, 0, :] - top), axis=0, keepdims=True)
    tgt_out[...] = 0.5 * (tp[...] + (tgt_bias - (top + jnp.log(total))))

    for k in range(1, blocks):
        peer = nearest(me, blocks, k)
        slot_copy(me, peer).wait_send()
        bias_copy(me, peer).wait_send()
        row_copy(me, peer).wait_send()
    for k in range(1, copies):
        col_copy(rep, (rep + k) % copies).wait_send()


def on_device(
    blocks, copies,
    src_spectra, tgt_spectra, log_src_weight, log_tgt_weight, src_potential, tgt_potential,
):
    bands, width = src_spectra.shape
    tgt_width = tgt_spectra.shape[1]
    depth = bands + EXTRA
    one = lambda vector: vector.reshape(1, -1)
    f32, bf16 = jnp.float32, jnp.bfloat16
    dma = pltpu.SemaphoreType.DMA
    elements = blocks * width * tgt_width
    src_updated, tgt_updated = pl.pallas_call(
        functools.partial(kernel, blocks, copies),
        out_shape=(
            jax.ShapeDtypeStruct((1, width), f32),
            jax.ShapeDtypeStruct((1, tgt_width), f32),
        ),
        in_specs=[pl.BlockSpec(memory_space=pl.ANY)] * 6,
        out_specs=(pl.BlockSpec(memory_space=pltpu.VMEM), pl.BlockSpec(memory_space=pltpu.VMEM)),
        scratch_shapes=[
            pltpu.VMEM((blocks, bands, width), bf16),
            pltpu.VMEM((blocks, 1, width), f32),
            pltpu.VMEM((bands, tgt_width), bf16),
            pltpu.VMEM((1, width), f32),
            pltpu.VMEM((1, tgt_width), f32),
            pltpu.VMEM((1, width), f32),
            pltpu.VMEM((1, tgt_width), f32),
            pltpu.VMEM((depth, tgt_width), bf16),
            pltpu.VMEM((tgt_width, depth), bf16),
            pltpu.VMEM((blocks, 2, width), f32),
            pltpu.VMEM((blocks, 2, width), f32),
            pltpu.VMEM((SUBLANES, tgt_width), f32),
            pltpu.VMEM((SUBLANES, tgt_width), f32),
            pltpu.VMEM((copies, 2, tgt_width), f32),
            dma((6,)),
            dma((blocks,)), dma((blocks,)),
            dma((blocks,)), dma((blocks,)),
            dma((blocks,)), dma((blocks,)),
            dma((copies,)), dma((copies,)),
        ],
        compiler_params=pltpu.CompilerParams(
            collective_id=0, has_side_effects=True, vmem_limit_bytes=32 * 1024 * 1024
        ),
        cost_estimate=pl.CostEstimate(
            flops=4 * elements * bands, bytes_accessed=4 * bands * tgt_width, transcendentals=2 * elements
        ),
        name="sinkhorn",
    )(
        src_spectra, tgt_spectra, one(log_src_weight), one(log_tgt_weight),
        one(src_potential), one(tgt_potential),
    )
    return src_updated.reshape(-1), tgt_updated.reshape(-1)


def solution(mesh):
    placed = (
        P(None, ("pair", "rep", "blk")),
        P(None, ("pair", "blk")),
        P(("pair", "rep", "blk")),
        P(("pair", "blk")),
        P(("pair", "rep", "blk")),
        P(("pair", "blk")),
    )
    return jax.shard_map(
        functools.partial(on_device, mesh.shape["blk"], mesh.shape["rep"]),
        mesh=mesh,
        in_specs=placed,
        out_specs=(P(("pair", "rep", "blk")), P(("pair", "blk"))),
        check_vma=False,
    )
```

time: 62.3 us -> 20.1 us (0.32)
  blocking collectives: 25.1 us -> 0 us
  waiting for transfers between devices: 16.1 us -> 0 us
  Pallas kernels: 0 us -> 15 us
  starting transfers between devices: 12.2 us -> 0 us
  other arithmetic: 3.3 us -> 0 us
  local copies, waits for them, and re-layouts: 2.21 us -> 4.19 us
  matrix products: 1.93 us -> 0 us
    all_gather x3 -> x0, blocking collectives: 25.1 us -> none  [the longest x1 14.8 us: on_device(): lax.all_gather(log_tgt_weight + tgt_potential, 'blk', axis=0, tiled=True)]
    ppermute x12 -> x0, waiting for transfers between devices: 16.1 us -> none  [passed_along(): return lax.ppermute(value, axis, pairs)]
    pallas_call x0 -> x1, Pallas kernels: none -> 15 us  [on_device(): pl.pallas_call(functools.partial(kernel, blocks, copies), out_shape=(jax....]
    ppermute x12 -> x0, starting transfers between devices: 12.2 us -> none  [passed_along(): return lax.ppermute(value, axis, pairs)]
    unnamed x14, local copies, waits for them, and re-layouts: 1.4 us -> 4.19 us
    reduce_sum x9 -> x0, other arithmetic: 1.93 us -> none  [the longest x4 1.74 us: column_part(): jnp.sum(jnp.exp(col_scores - block_peak[None, :]), axis=0)]
    dot_general x4 -> x0, matrix products: 1.93 us -> none  [tile_scores(): lax.dot_general(src_spectra, spectra_piece, (((0,), (0,)), ((), ())), pre...]
    mul x7 -> x0, other arithmetic: 1.2 us -> none  [the longest x2 1.18 us: on_device(): return (0.5 * (src_potential + src_new), 0.5 * (tgt_potential + tgt_new))]
  transfers between devices with their start and end apart: 12 -> 0, of which waited for: 8 -> 0; matrix products, arithmetic and copies ran while one was open for 6% -> 0% of each run, Pallas kernels for 0% -> 0%
where the time goes in v1:
time: 20.1 us; the launch traced here: 19.8 us
  Pallas kernels  15 us (75%)
  local copies, waits for them, and re-layouts  4.19 us (21%)
  between operations  0.67 us (3%)
    pallas_call x1, Pallas kernels, on_device(): pl.pallas_call(functools.partial(kernel, blocks, copies), out_shape=(jax....  15 us
    unnamed x14, local copies, waits for them, and re-layouts  4.19 us

profile of v1, /device:TPU:0, one launch (start us, length us, event | category | flops | bytes accessed | tf_op | source)
XLA Modules:
  0.0 19.8 jit_solution(972609794709239741)
XLA Ops:
  0.6 0.0 copy-start.2
  0.6 0.0 copy-start.5
  0.7 0.0 copy-start.4
  0.7 0.7 %copy-done.2 = f32[1024]{0:T(1024)S(1)} copy-done((f32[1024]{0:T(1024)S(1)}, f32[1024]{0:T(1024)}, u32[]{:S(2)}) %copy-start.2) | copy-done | bytes 4120
  1.3 0.0 copy-done.5
  1.3 0.0 copy-done.4
  1.3 0.0 copy-start
  1.3 0.9 %copy-done = bf16[64,1024]{1,0:T(8,128)(2,1)S(1)} copy-done((bf16[64,1024]{1,0:T(8,128)(2,1)S(1)}, bf16[64,1024]{1,0:T(8,128)(2,1)}, u32[]{:S(2)}) %copy-start) | copy-done | bytes 131096
  2.2 0.0 copy-start.1
  2.2 0.8 %copy-done.1 = bf16[64,256]{1,0:T(8,128)(2,1)S(1)} copy-done((bf16[64,256]{1,0:T(8,128)(2,1)S(1)}, bf16[64,256]{1,0:T(8,128)(2,1)}, u32[]{:S(2)}) %copy-start.1) | copy-done | bytes 32792
  3.0 0.0 copy-start.3
  3.0 0.7 %copy-done.3 = f32[1024]{0:T(1024)S(1)} copy-done((f32[1024]{0:T(1024)S(1)}, f32[1024]{0:T(1024)}, u32[]{:S(2)}) %copy-start.3) | copy-done | bytes 4120
  3.7 15.0 %sinkhorn.1 = (f32[1,256]{1,0:T(1,128)S(1)}, f32[1,1024]{1,0:T(1,128)S(1)}) custom-call(bf16[64,256]{1,0:T(8,128)(2,1)S(1)} %copy-done.1, bf16[64,1024]{1,0:T(8,128)(2,1)S(1)} %copy-done, f32[1,256]{1,0:T(1,128)S(1)} %bitcast.10, f32[1,1024]{1,0:T(1,128)S(1)} %bitcast.8, f32[1,256]{1,0:T(1,128)S(1)} %bitcast.11, f32[1,1024]{1,0:T(1,128)S(1)} %bitcast.9), custom_call_target="tpu_custom_call" | custom-call | flops 268435456 | bytes 262144 | tf_op jit(solution)/shard_map/sinkhorn/pallas_call | solution.py:223
  18.7 0.6 %copy.10 = f32[256]{0:T(256)} copy(f32[256]{0:T(256)S(1)} %bitcast.7) | data formatting | bytes 2048
  19.3 0.6 %copy.11 = f32[1024]{0:T(1024)} copy(f32[1024]{0:T(1024)S(1)} %bitcast.6) | data formatting | bytes 8192
Async XLA Ops:
  0.6 0.7 %copy-start.2 = (f32[1024]{0:T(1024)S(1)}, f32[1024]{0:T(1024)}, u32[]{:S(2)}) copy-start(f32[1024]{0:T(1024)} %param.9) | copy-start | bytes 12292
  0.6 0.7 %copy-start.5 = (f32[256]{0:T(256)S(1)}, f32[256]{0:T(256)}, u32[]{:S(2)}) copy-start(f32[256]{0:T(256)} %param.10) | copy-start | bytes 3076
  0.7 0.7 %copy-start.4 = (f32[256]{0:T(256)S(1)}, f32[256]{0:T(256)}, u32[]{:S(2)}) copy-start(f32[256]{0:T(256)} %param.8) | copy-start | bytes 3076
  1.3 0.9 %copy-start = (bf16[64,1024]{1,0:T(8,128)(2,1)S(1)}, bf16[64,1024]{1,0:T(8,128)(2,1)}, u32[]{:S(2)}) copy-start(bf16[64,1024]{1,0:T(8,128)(2,1)} %tgt_hbm.1) | copy-start | bytes 393220
  2.2 0.8 %copy-start.1 = (bf16[64,256]{1,0:T(8,128)(2,1)S(1)}, bf16[64,256]{1,0:T(8,128)(2,1)}, u32[]{:S(2)}) copy-start(bf16[64,256]{1,0:T(8,128)(2,1)} %src_hbm.1) | copy-start | bytes 98308
  3.0 0.7 %copy-start.3 = (f32[1024]{0:T(1024)S(1)}, f32[1024]{0:T(1024)}, u32[]{:S(2)}) copy-start(f32[1024]{0:T(1024)} %param.11) | copy-start | bytes 12292

commit v2 on v1

--- a/solution.py
+++ b/solution.py
@@ -10,6 +10,7 @@
 MESH = pl.DeviceIdType.MESH
 SUBLANES = 8
 EXTRA = 16
+DEPTH = 128
 TILE = 256
 
 
@@ -43,11 +44,9 @@
     return 0.5 * jnp.sum(wide * wide, axis=0, keepdims=True)
 
 
-def peak_and_sum(scores):
+def by_sublane(scores):
     rows, width = scores.shape
-    grouped = scores.reshape(rows // SUBLANES, SUBLANES, width)
-    peak = jnp.max(grouped, axis=0)
-    return peak, jnp.sum(jnp.exp(grouped - peak[None]), axis=0)
+    return scores.reshape(rows // SUBLANES, SUBLANES, width)
 
 
 def joined(earlier, later):
@@ -64,7 +63,7 @@
     blocks, copies,
     src_hbm, tgt_hbm, lsw_hbm, ltw_hbm, sp_hbm, tp_hbm,
     src_out, tgt_out,
-    slots, biases, tgt_v, lsw, ltw, sp, tp, tgt_flat, tgt_tall, row_mine, row_stats, col_peak, col_total,
+    slots, biases, tgt_v, lsw, ltw, sp, tp, tgt_flat, tgt_tall, scores, row_mine, row_stats, col_peak, col_total,
     col_stats,
     load_sem, slot_send, slot_recv, bias_send, bias_recv, row_send, row_recv, col_send, col_recv,
 ):
@@ -72,6 +71,7 @@
     rep = lax.axis_index("rep")
     bands, width = src_hbm.shape
     tgt_width = tgt_hbm.shape[1]
+    depth = tgt_flat.shape[0]
 
     barrier = pltpu.get_barrier_semaphore()
     for k in range(1, blocks):
@@ -134,6 +134,10 @@
         load.wait()
     tgt_bias = ltw[...] + tp[...]
     tgt_flat[pl.ds(0, bands), :] = tgt_v[...]
+    if depth > bands + EXTRA:
+        tgt_flat[pl.ds(bands + EXTRA, depth - bands - EXTRA), :] = jnp.zeros(
+            (depth - bands - EXTRA, tgt_width), jnp.bfloat16
+        )
     tgt_flat[pl.ds(bands, EXTRA), :] = bias_rows(tgt_bias - half_square(tgt_v[...]), 3)
     for at in range(0, tgt_width, TILE):
         tgt_tall[pl.ds(at, TILE), :] = tgt_flat[:, pl.ds(at, TILE)].T
@@ -148,23 +152,42 @@
             slot_copy(place, place).wait_recv()
             bias_copy(place, place).wait_recv()
 
-        src = jnp.concatenate([slots[place], bias_rows(biases[place], 0)], axis=0)
+        src = [slots[place], bias_rows(biases[place], 0)]
+        if depth > bands + EXTRA:
+            src.append(jnp.zeros((depth - bands - EXTRA, width), jnp.bfloat16))
+        src = jnp.concatenate(src, axis=0)
         src_tall = src.T
-        row = None
+        parts = []
+
+        def finish(peak, slot, at, down):
+            total = jnp.sum(jnp.exp(by_sublane(scores[slot]) - peak[None]), axis=0)
+            if down:
+                here = (slice(None), pl.ds(at, TILE))
+                col_peak[here], col_total[here] = joined(
+                    (col_peak[here], col_total[here]), (peak, total)
+                )
+            else:
+                parts.append((peak, total))
+
+        waiting = None
         for at in range(0, tgt_width, TILE):
-            across = jnp.dot(
-                tgt_tall[pl.ds(at, TILE), :], src, preferred_element_type=jnp.float32
-            )
-            part = peak_and_sum(across)
-            row = part if row is None else joined(row, part)
-            down = jnp.dot(
-                src_tall, tgt_flat[:, pl.ds(at, TILE)], preferred_element_type=jnp.float32
-            )
-            here = (slice(None), pl.ds(at, TILE))
-            col_peak[here], col_total[here] = joined(
-                (col_peak[here], col_total[here]), peak_and_sum(down)
-            )
-        top, total = folded(*row)
+            for down in (False, True):
+                if down:
+                    block = jnp.dot(
+                        src_tall, tgt_flat[:, pl.ds(at, TILE)], preferred_element_type=jnp.float32
+                    )
+                else:
+                    block = jnp.dot(
+                        tgt_tall[pl.ds(at, TILE), :], src, preferred_element_type=jnp.float32
+                    )
+                slot = 2 * (at // TILE) + down
+                scores[slot] = block
+                peak = jnp.max(by_sublane(block), axis=0)
+                if waiting is not None:
+                    finish(*waiting)
+                waiting = (peak, slot, at, down)
+        finish(*waiting)
+        top, total = folded(*functools.reduce(joined, parts))
         stats = jnp.concatenate([top, total], axis=0)
 
         @pl.when(k > 0)
@@ -209,24 +232,32 @@
         col_copy(rep, (rep + k) % copies).wait_send()
 
 
+def write_out(src, tgt, src_out, tgt_out, sem):
+    copies = [
+        pltpu.make_async_copy(src, src_out, sem.at[0]),
+        pltpu.make_async_copy(tgt, tgt_out, sem.at[1]),
+    ]
+    for copy in copies:
+        copy.start()
+    for copy in copies:
+        copy.wait()
+
+
 def on_device(
     blocks, copies,
     src_spectra, tgt_spectra, log_src_weight, log_tgt_weight, src_potential, tgt_potential,
 ):
     bands, width = src_spectra.shape
     tgt_width = tgt_spectra.shape[1]
-    depth = bands + EXTRA
+    depth = -(-(bands + EXTRA) // DEPTH) * DEPTH
     one = lambda vector: vector.reshape(1, -1)
     f32, bf16 = jnp.float32, jnp.bfloat16
     dma = pltpu.SemaphoreType.DMA
     elements = blocks * width * tgt_width
     src_updated, tgt_updated = pl.pallas_call(
         functools.partial(kernel, blocks, copies),
-        out_shape=(
-            jax.ShapeDtypeStruct((1, width), f32),
-            jax.ShapeDtypeStruct((1, tgt_width), f32),
-        ),
-        in_specs=[pl.BlockSpec(memory_space=pl.ANY)] * 6,
+        out_shape=(pltpu.VMEM((1, width), f32), pltpu.VMEM((1, tgt_width), f32)),
+        in_specs=[pl.BlockSpec(memory_space=pltpu.HBM)] * 6,
         out_specs=(pl.BlockSpec(memory_space=pltpu.VMEM), pl.BlockSpec(memory_space=pltpu.VMEM)),
         scratch_shapes=[
             pltpu.VMEM((blocks, bands, width), bf16),
@@ -238,6 +269,7 @@
             pltpu.VMEM((1, tgt_width), f32),
             pltpu.VMEM((depth, tgt_width), bf16),
             pltpu.VMEM((tgt_width, depth), bf16),
+            pltpu.VMEM((2 * tgt_width // TILE, TILE, TILE), f32),
             pltpu.VMEM((blocks, 2, width), f32),
             pltpu.VMEM((blocks, 2, width), f32),
             pltpu.VMEM((SUBLANES, tgt_width), f32),
@@ -257,9 +289,25 @@
         ),
         name="sinkhorn",
     )(
-        src_spectra, tgt_spectra, one(log_src_weight), one(log_tgt_weight),
-        one(src_potential), one(tgt_potential),
+        *(
+            pltpu.with_memory_space_constraint(array, pltpu.HBM)
+            for array in (
+                src_spectra, tgt_spectra, one(log_src_weight), one(log_tgt_weight),
+                one(src_potential), one(tgt_potential),
+            )
+        )
     )
+    src_updated, tgt_updated = pl.pallas_call(
+        write_out,
+        out_shape=(
+            jax.ShapeDtypeStruct((1, width), f32),
+            jax.ShapeDtypeStruct((1, tgt_width), f32),
+        ),
+        in_specs=[pl.BlockSpec(memory_space=pltpu.VMEM)] * 2,
+        out_specs=(pl.BlockSpec(memory_space=pltpu.HBM), pl.BlockSpec(memory_space=pltpu.HBM)),
+        scratch_shapes=[dma((2,))],
+        name="write_out",
+    )(src_updated, tgt_updated)
     return src_updated.reshape(-1), tgt_updated.reshape(-1)
 
 

time: 20.1 us -> 18.5 us (0.920)
  local copies, waits for them, and re-layouts: 4.19 us -> 1.13 us
  Pallas kernels: 15 us -> 16.5 us
    unnamed x14 -> x4, local copies, waits for them, and re-layouts: 4.19 us -> 1.13 us
    pallas_call x1 -> x2, Pallas kernels: 15 us -> 16.5 us  [the longest x1 15.3 us: on_device(): pl.pallas_call(functools.partial(kernel, blocks, copies), out_shape=(pltp...]
where the time goes in v2:
time: 18.5 us; the launch traced here: 18.3 us
  Pallas kernels  16.5 us (89%)
  local copies, waits for them, and re-layouts  1.13 us (6%)
  between operations  0.65 us (4%)
    pallas_call x1, Pallas kernels, on_device(): pl.pallas_call(functools.partial(kernel, blocks, copies), out_shape=(pltp...  15.3 us
    pallas_call x1, Pallas kernels, on_device(): pl.pallas_call(write_out, out_shape=(jax.ShapeDtypeStruct((1, width), f32...  1.29 us
    unnamed x4, local copies, waits for them, and re-layouts  1.13 us

profile of v2, /device:TPU:0, one launch (start us, length us, event | category | flops | bytes accessed | tf_op | source)
XLA Modules:
  0.0 18.3 jit_solution(11551591323378584404)
XLA Ops:
  0.6 15.3 %sinkhorn.1 = (f32[1,256]{1,0:T(1,128)S(1)}, f32[1,1024]{1,0:T(1,128)S(1)}) custom-call(bf16[64,256]{1,0:T(8,128)(2,1)} %src_hbm.1, bf16[64,1024]{1,0:T(8,128)(2,1)} %tgt_hbm.1, f32[1,256]{1,0:T(1,128)} %bitcast.9, f32[1,1024]{1,0:T(1,128)} %bitcast.6, f32[1,256]{1,0:T(1,128)} %bitcast.10, f32[1,1024]{1,0:T(1,128)} %bitcast.7), custom_call_target="tpu_custom_call" | custom-call | flops 268435456 | bytes 262144 | tf_op jit(solution)/shard_map/sinkhorn/pallas_call | solution.py:257
  15.9 0.0 copy-start
  15.9 0.6 %copy-done = f32[1,1024]{1,0:T(1,128)} copy-done((f32[1,1024]{1,0:T(1,128)}, f32[1,1024]{1,0:T(1,128)S(1)}, u32[]{:S(2)}) %copy-start) | copy-done | bytes 4120
  16.5 0.0 copy-start.1
  16.5 0.5 %copy-done.1 = f32[1,256]{1,0:T(1,128)} copy-done((f32[1,256]{1,0:T(1,128)}, f32[1,256]{1,0:T(1,128)S(1)}, u32[]{:S(2)}) %copy-start.1) | copy-done | bytes 1048
  17.0 1.3 %write_out.1 = (f32[1,256]{1,0:T(1,128)}, f32[1,1024]{1,0:T(1,128)}) custom-call(f32[1,256]{1,0:T(1,128)} %copy-done.1, f32[1,1024]{1,0:T(1,128)} %copy-done), custom_call_target="tpu_custom_call" | custom-call | tf_op jit(solution)/shard_map/write_out/pallas_call | solution.py:300
Async XLA Ops:
  15.9 0.6 %copy-start = (f32[1,1024]{1,0:T(1,128)}, f32[1,1024]{1,0:T(1,128)S(1)}, u32[]{:S(2)}) copy-start(f32[1,1024]{1,0:T(1,128)S(1)} %get-tuple-element.7.tgt) | copy-start | bytes 12292
  16.5 0.5 %copy-start.1 = (f32[1,256]{1,0:T(1,128)}, f32[1,256]{1,0:T(1,128)S(1)}, u32[]{:S(2)}) copy-start(f32[1,256]{1,0:T(1,128)S(1)} %get-tuple-element.6.src) | copy-start | bytes 3076

commit v3 on v1

--- a/solution.py
+++ b/solution.py
@@ -9,7 +9,9 @@
 
 MESH = pl.DeviceIdType.MESH
 SUBLANES = 8
+WIDE = 32
 EXTRA = 16
+DEPTH = 128
 TILE = 256
 
 
@@ -43,11 +45,9 @@
     return 0.5 * jnp.sum(wide * wide, axis=0, keepdims=True)
 
 
-def peak_and_sum(scores):
+def grouped(scores, group):
     rows, width = scores.shape
-    grouped = scores.reshape(rows // SUBLANES, SUBLANES, width)
-    peak = jnp.max(grouped, axis=0)
-    return peak, jnp.sum(jnp.exp(grouped - peak[None]), axis=0)
+    return scores.reshape(rows // group, group, width)
 
 
 def joined(earlier, later):
@@ -64,7 +64,7 @@
     blocks, copies,
     src_hbm, tgt_hbm, lsw_hbm, ltw_hbm, sp_hbm, tp_hbm,
     src_out, tgt_out,
-    slots, biases, tgt_v, lsw, ltw, sp, tp, tgt_flat, tgt_tall, row_mine, row_stats, col_peak, col_total,
+    slots, biases, tgt_v, lsw, ltw, sp, tp, tgt_flat, tgt_tall, across, down, row_mine, row_stats, col_peak, col_total,
     col_stats,
     load_sem, slot_send, slot_recv, bias_send, bias_recv, row_send, row_recv, col_send, col_recv,
 ):
@@ -72,6 +72,7 @@
     rep = lax.axis_index("rep")
     bands, width = src_hbm.shape
     tgt_width = tgt_hbm.shape[1]
+    depth = tgt_flat.shape[0]
 
     barrier = pltpu.get_barrier_semaphore()
     for k in range(1, blocks):
@@ -134,6 +135,10 @@
         load.wait()
     tgt_bias = ltw[...] + tp[...]
     tgt_flat[pl.ds(0, bands), :] = tgt_v[...]
+    if depth > bands + EXTRA:
+        tgt_flat[pl.ds(bands + EXTRA, depth - bands - EXTRA), :] = jnp.zeros(
+            (depth - bands - EXTRA, tgt_width), jnp.bfloat16
+        )
     tgt_flat[pl.ds(bands, EXTRA), :] = bias_rows(tgt_bias - half_square(tgt_v[...]), 3)
     for at in range(0, tgt_width, TILE):
         tgt_tall[pl.ds(at, TILE), :] = tgt_flat[:, pl.ds(at, TILE)].T
@@ -148,23 +153,32 @@
             slot_copy(place, place).wait_recv()
             bias_copy(place, place).wait_recv()
 
-        src = jnp.concatenate([slots[place], bias_rows(biases[place], 0)], axis=0)
+        src = [slots[place], bias_rows(biases[place], 0)]
+        if depth > bands + EXTRA:
+            src.append(jnp.zeros((depth - bands - EXTRA, width), jnp.bfloat16))
+        src = jnp.concatenate(src, axis=0)
         src_tall = src.T
-        row = None
-        for at in range(0, tgt_width, TILE):
-            across = jnp.dot(
-                tgt_tall[pl.ds(at, TILE), :], src, preferred_element_type=jnp.float32
-            )
-            part = peak_and_sum(across)
-            row = part if row is None else joined(row, part)
-            down = jnp.dot(
+        tiles = range(0, tgt_width, TILE)
+        row_peak = None
+        for at in tiles:
+            block = jnp.dot(tgt_tall[pl.ds(at, TILE), :], src, preferred_element_type=jnp.float32)
+            across[pl.ds(at, TILE), :] = block
+            peak = jnp.max(grouped(block, WIDE), axis=0)
+            row_peak = peak if row_peak is None else jnp.maximum(row_peak, peak)
+        col_peaks = []
+        for at in tiles:
+            block = jnp.dot(
                 src_tall, tgt_flat[:, pl.ds(at, TILE)], preferred_element_type=jnp.float32
             )
-            here = (slice(None), pl.ds(at, TILE))
-            col_peak[here], col_total[here] = joined(
-                (col_peak[here], col_total[here]), peak_and_sum(down)
-            )
-        top, total = folded(*row)
+            down[:, pl.ds(at, TILE)] = block
+            peak = jnp.max(grouped(block, WIDE), axis=0)
+            col_peaks.append(jnp.max(grouped(peak, SUBLANES), axis=0))
+        row_total = None
+        for at in tiles:
+            block = grouped(across[pl.ds(at, TILE), :], WIDE)
+            total = jnp.sum(jnp.exp(block - row_peak[None]), axis=0)
+            row_total = total if row_total is None else row_total + total
+        top, total = folded(row_peak, row_total)
         stats = jnp.concatenate([top, total], axis=0)
 
         @pl.when(k > 0)
@@ -176,6 +190,14 @@
         def _():
             row_stats[me] = stats
 
+        for at, peak in zip(tiles, col_peaks):
+            here = (slice(None), pl.ds(at, TILE))
+            terms = jnp.exp(grouped(down[here], SUBLANES) - peak[None])
+            total = jnp.sum(terms.reshape(-1, WIDE, TILE), axis=0)
+            total = jnp.sum(grouped(total, SUBLANES), axis=0)
+            col_peak[here], col_total[here] = joined(
+                (col_peak[here], col_total[here]), (peak, total)
+            )
         return carry
 
     lax.fori_loop(0, blocks, turn, 0)
@@ -215,18 +237,15 @@
 ):
     bands, width = src_spectra.shape
     tgt_width = tgt_spectra.shape[1]
-    depth = bands + EXTRA
+    depth = -(-(bands + EXTRA) // DEPTH) * DEPTH
     one = lambda vector: vector.reshape(1, -1)
     f32, bf16 = jnp.float32, jnp.bfloat16
     dma = pltpu.SemaphoreType.DMA
     elements = blocks * width * tgt_width
     src_updated, tgt_updated = pl.pallas_call(
         functools.partial(kernel, blocks, copies),
-        out_shape=(
-            jax.ShapeDtypeStruct((1, width), f32),
-            jax.ShapeDtypeStruct((1, tgt_width), f32),
-        ),
-        in_specs=[pl.BlockSpec(memory_space=pl.ANY)] * 6,
+        out_shape=(pltpu.VMEM((1, width), f32), pltpu.VMEM((1, tgt_width), f32)),
+        in_specs=[pl.BlockSpec(memory_space=pltpu.HBM)] * 6,
         out_specs=(pl.BlockSpec(memory_space=pltpu.VMEM), pl.BlockSpec(memory_space=pltpu.VMEM)),
         scratch_shapes=[
             pltpu.VMEM((blocks, bands, width), bf16),
@@ -238,6 +257,8 @@
             pltpu.VMEM((1, tgt_width), f32),
             pltpu.VMEM((depth, tgt_width), bf16),
             pltpu.VMEM((tgt_width, depth), bf16),
+            pltpu.VMEM((tgt_width, width), f32),
+            pltpu.VMEM((width, tgt_width), f32),
             pltpu.VMEM((blocks, 2, width), f32),
             pltpu.VMEM((blocks, 2, width), f32),
             pltpu.VMEM((SUBLANES, tgt_width), f32),
@@ -257,8 +278,13 @@
         ),
         name="sinkhorn",
     )(
-        src_spectra, tgt_spectra, one(log_src_weight), one(log_tgt_weight),
-        one(src_potential), one(tgt_potential),
+        *(
+            pltpu.with_memory_space_constraint(array, pltpu.HBM)
+            for array in (
+                src_spectra, tgt_spectra, one(log_src_weight), one(log_tgt_weight),
+                one(src_potential), one(tgt_potential),
+            )
+        )
     )
     return src_updated.reshape(-1), tgt_updated.reshape(-1)
 

time: 20.1 us -> 17.1 us (0.85)
  local copies, waits for them, and re-layouts: 4.19 us -> 1.16 us
    unnamed x14 -> x2, local copies, waits for them, and re-layouts: 4.19 us -> 1.16 us
where the time goes in v3:
time: 17.1 us; the launch traced here: 16.9 us
  Pallas kernels  15.1 us (88%)
  local copies, waits for them, and re-layouts  1.16 us (7%)
  between operations  0.64 us (4%)
    pallas_call x1, Pallas kernels, on_device(): pl.pallas_call(functools.partial(kernel, blocks, copies), out_shape=(pltp...  15.1 us
    unnamed x2, local copies, waits for them, and re-layouts  1.16 us

profile of v3, /device:TPU:0, one launch (start us, length us, event | category | flops | bytes accessed | tf_op | source)
XLA Modules:
  0.0 16.9 jit_solution(9304219391723038950)
XLA Ops:
  0.6 15.1 %sinkhorn.1 = (f32[1,256]{1,0:T(1,128)S(1)}, f32[1,1024]{1,0:T(1,128)S(1)}) custom-call(bf16[64,256]{1,0:T(8,128)(2,1)} %src_hbm.1, bf16[64,1024]{1,0:T(8,128)(2,1)} %tgt_hbm.1, f32[1,256]{1,0:T(1,128)} %bitcast.10, f32[1,1024]{1,0:T(1,128)} %bitcast.8, f32[1,256]{1,0:T(1,128)} %bitcast.11, f32[1,1024]{1,0:T(1,128)} %bitcast.9), custom_call_target="tpu_custom_call" | custom-call | flops 268435456 | bytes 262144 | tf_op jit(solution)/shard_map/sinkhorn/pallas_call | solution.py:245
  15.8 0.6 %copy.10 = f32[256]{0:T(256)} copy(f32[256]{0:T(256)S(1)} %bitcast.7) | data formatting | bytes 2048
  16.3 0.6 %copy.11 = f32[1024]{0:T(1024)} copy(f32[1024]{0:T(1024)S(1)} %bitcast.6) | data formatting | bytes 8192

commit v4 on v3

--- a/solution.py
+++ b/solution.py
@@ -64,9 +64,9 @@
     blocks, copies,
     src_hbm, tgt_hbm, lsw_hbm, ltw_hbm, sp_hbm, tp_hbm,
     src_out, tgt_out,
-    slots, biases, tgt_v, lsw, ltw, sp, tp, tgt_flat, tgt_tall, across, down, row_mine, row_stats, col_peak, col_total,
+    slots, lsw, sp, tgt_v, ltw, tp, tgt_flat, tgt_tall, across, down, row_mine, row_stats, col_peak, col_total,
     col_stats,
-    load_sem, slot_send, slot_recv, bias_send, bias_recv, row_send, row_recv, col_send, col_recv,
+    load_sem, slot_send, slot_recv, row_send, row_recv, col_send, col_recv,
 ):
     me = lax.axis_index("blk")
     rep = lax.axis_index("rep")
@@ -85,8 +85,8 @@
         )
     loads = [
         pltpu.make_async_copy(src_hbm, slots.at[me], load_sem.at[0]),
-        pltpu.make_async_copy(lsw_hbm, lsw, load_sem.at[1]),
-        pltpu.make_async_copy(sp_hbm, sp, load_sem.at[2]),
+        pltpu.make_async_copy(lsw_hbm, lsw.at[me], load_sem.at[1]),
+        pltpu.make_async_copy(sp_hbm, sp.at[me], load_sem.at[2]),
         pltpu.make_async_copy(tgt_hbm, tgt_v, load_sem.at[3]),
         pltpu.make_async_copy(ltw_hbm, ltw, load_sem.at[4]),
         pltpu.make_async_copy(tp_hbm, tp, load_sem.at[5]),
@@ -95,19 +95,15 @@
         load.start()
     pl.semaphore_wait(barrier, blocks + copies - 2)
 
-    def slot_copy(place, peer):
-        return pltpu.make_async_remote_copy(
-            src_ref=src_hbm, dst_ref=slots.at[place],
-            send_sem=slot_send.at[peer], recv_sem=slot_recv.at[place],
-            device_id={"blk": peer}, device_id_type=MESH,
-        )
-
-    def bias_copy(place, peer):
-        return pltpu.make_async_remote_copy(
-            src_ref=biases.at[me], dst_ref=biases.at[place],
-            send_sem=bias_send.at[peer], recv_sem=bias_recv.at[place],
-            device_id={"blk": peer}, device_id_type=MESH,
-        )
+    def source_copies(place, peer):
+        return [
+            pltpu.make_async_remote_copy(
+                src_ref=source, dst_ref=target.at[place],
+                send_sem=slot_send.at[at, peer], recv_sem=slot_recv.at[at, place],
+                device_id={"blk": peer}, device_id_type=MESH,
+            )
+            for at, (source, target) in enumerate(((src_hbm, slots), (lsw_hbm, lsw), (sp_hbm, sp)))
+        ]
 
     def row_copy(place, peer):
         return pltpu.make_async_remote_copy(
@@ -123,15 +119,10 @@
             device_id={"rep": peer}, device_id_type=MESH,
         )
 
-    for k in range(1, blocks):
-        slot_copy(me, nearest(me, blocks, k)).start()
-    for load in loads[:3]:
-        load.wait()
-    src_bias = lsw[...] + sp[...]
-    biases[me] = src_bias - half_square(slots[me])
-    for k in range(1, blocks):
-        bias_copy(me, nearest(me, blocks, k)).start()
-    for load in loads[3:]:
+    for k in reversed(range(1, blocks)):
+        for copy in source_copies(me, nearest(me, blocks, k)):
+            copy.start()
+    for load in loads:
         load.wait()
     tgt_bias = ltw[...] + tp[...]
     tgt_flat[pl.ds(0, bands), :] = tgt_v[...]
@@ -150,10 +141,11 @@
 
         @pl.when(k > 0)
         def _():
-            slot_copy(place, place).wait_recv()
-            bias_copy(place, place).wait_recv()
-
-        src = [slots[place], bias_rows(biases[place], 0)]
+            for copy in source_copies(place, place):
+                copy.wait_recv()
+
+        block = slots[place]
+        src = [block, bias_rows(lsw[place] + sp[place] - half_square(block), 0)]
         if depth > bands + EXTRA:
             src.append(jnp.zeros((depth - bands - EXTRA, width), jnp.bfloat16))
         src = jnp.concatenate(src, axis=0)
@@ -212,7 +204,7 @@
     every = row_stats[...]
     top = jnp.max(every[:, 0, :], axis=0, keepdims=True)
     total = jnp.sum(every[:, 1, :] * jnp.exp(every[:, 0, :] - top), axis=0, keepdims=True)
-    src_out[...] = 0.5 * (sp[...] + (src_bias - (top + jnp.log(total))))
+    src_out[...] = 0.5 * (sp[me] + (lsw[me] + sp[me] - (top + jnp.log(total))))
 
     for k in range(1, copies):
         place = (rep + k) % copies
@@ -224,8 +216,8 @@
 
     for k in range(1, blocks):
         peer = nearest(me, blocks, k)
-        slot_copy(me, peer).wait_send()
-        bias_copy(me, peer).wait_send()
+        for copy in source_copies(me, peer):
+            copy.wait_send()
         row_copy(me, peer).wait_send()
     for k in range(1, copies):
         col_copy(rep, (rep + k) % copies).wait_send()
@@ -250,10 +242,9 @@
         scratch_shapes=[
             pltpu.VMEM((blocks, bands, width), bf16),
             pltpu.VMEM((blocks, 1, width), f32),
+            pltpu.VMEM((blocks, 1, width), f32),
             pltpu.VMEM((bands, tgt_width), bf16),
-            pltpu.VMEM((1, width), f32),
             pltpu.VMEM((1, tgt_width), f32),
-            pltpu.VMEM((1, width), f32),
             pltpu.VMEM((1, tgt_width), f32),
             pltpu.VMEM((depth, tgt_width), bf16),
             pltpu.VMEM((tgt_width, depth), bf16),
@@ -265,8 +256,7 @@
             pltpu.VMEM((SUBLANES, tgt_width), f32),
             pltpu.VMEM((copies, 2, tgt_width), f32),
             dma((6,)),
-            dma((blocks,)), dma((blocks,)),
-            dma((blocks,)), dma((blocks,)),
+            dma((3, blocks)), dma((3, blocks)),
             dma((blocks,)), dma((blocks,)),
             dma((copies,)), dma((copies,)),
         ],

time: 17.1 us -> 16.8 us (0.982)
  Pallas kernels: 15.1 us -> 14.9 us
    pallas_call x1, Pallas kernels: 15.1 us -> 14.9 us  [on_device(): pl.pallas_call(functools.partial(kernel, blocks, copies), out_shape=(pltp...]
where the time goes in v4:
time: 16.8 us; the launch traced here: 16.7 us
  Pallas kernels  14.9 us (89%)
  local copies, waits for them, and re-layouts  1.16 us (7%)
  between operations  0.64 us (4%)
    pallas_call x1, Pallas kernels, on_device(): pl.pallas_call(functools.partial(kernel, blocks, copies), out_shape=(pltp...  14.9 us
    unnamed x2, local copies, waits for them, and re-layouts  1.16 us

profile of v4, /device:TPU:0, one launch (start us, length us, event | category | flops | bytes accessed | tf_op | source)
XLA Modules:
  0.0 16.7 jit_solution(671635231995550208)
XLA Ops:
  0.6 14.9 %sinkhorn.1 = (f32[1,256]{1,0:T(1,128)S(1)}, f32[1,1024]{1,0:T(1,128)S(1)}) custom-call(bf16[64,256]{1,0:T(8,128)(2,1)} %src_hbm.1, bf16[64,1024]{1,0:T(8,128)(2,1)} %tgt_hbm.1, f32[1,256]{1,0:T(1,128)} %bitcast.10, f32[1,1024]{1,0:T(1,128)} %bitcast.8, f32[1,256]{1,0:T(1,128)} %bitcast.11, f32[1,1024]{1,0:T(1,128)} %bitcast.9), custom_call_target="tpu_custom_call" | custom-call | flops 268435456 | bytes 262144 | tf_op jit(solution)/shard_map/sinkhorn/pallas_call | solution.py:237
  15.5 0.6 %copy.10 = f32[256]{0:T(256)} copy(f32[256]{0:T(256)S(1)} %bitcast.7) | data formatting | bytes 2048
  16.1 0.6 %copy.11 = f32[1024]{0:T(1024)} copy(f32[1024]{0:T(1024)S(1)} %bitcast.6) | data formatting | bytes 8192

commit v5 on v4

--- a/solution.py
+++ b/solution.py
@@ -30,13 +30,15 @@
     return high, middle, value - high - middle
 
 
-def bias_rows(value, first):
-    high, middle, low = in_three(value)
-    row = lax.broadcasted_iota(jnp.int32, (EXTRA, value.shape[1]), 0)
-    out = jnp.where(row < 6, 1.0, 0.0)
-    out = jnp.where(row == first, high, out)
-    out = jnp.where(row == first + 1, middle, out)
-    out = jnp.where(row == first + 2, low, out)
+def bias_rows(value, width, first=0):
+    row = lax.broadcasted_iota(jnp.int32, (EXTRA, width), 0)
+    other = 3 - first
+    out = jnp.where((row >= other) & (row < other + 3), 1.0, 0.0)
+    if value is not None:
+        high, middle, low = in_three(value)
+        out = jnp.where(row == first, high, out)
+        out = jnp.where(row == first + 1, middle, out)
+        out = jnp.where(row == first + 2, low, out)
     return out.astype(jnp.bfloat16)
 
 
@@ -130,12 +132,22 @@
         tgt_flat[pl.ds(bands + EXTRA, depth - bands - EXTRA), :] = jnp.zeros(
             (depth - bands - EXTRA, tgt_width), jnp.bfloat16
         )
-    tgt_flat[pl.ds(bands, EXTRA), :] = bias_rows(tgt_bias - half_square(tgt_v[...]), 3)
+    tgt_flat[pl.ds(bands, EXTRA), :] = bias_rows(
+        tgt_bias - half_square(tgt_v[...]), tgt_width, 3
+    )
     for at in range(0, tgt_width, TILE):
         tgt_tall[pl.ds(at, TILE), :] = tgt_flat[:, pl.ds(at, TILE)].T
     col_peak[...] = jnp.full_like(col_peak, -jnp.inf)
     col_total[...] = jnp.zeros_like(col_total)
 
+    src_square = half_square(slots[me])
+
+    def deepened(block, extra):
+        pieces = [block, extra]
+        if depth > bands + EXTRA:
+            pieces.append(jnp.zeros((depth - bands - EXTRA, width), jnp.bfloat16))
+        return jnp.concatenate(pieces, axis=0)
+
     def turn(k, carry):
         place = nearest(me, blocks, k)
 
@@ -144,12 +156,9 @@
             for copy in source_copies(place, place):
                 copy.wait_recv()
 
-        block = slots[place]
-        src = [block, bias_rows(lsw[place] + sp[place] - half_square(block), 0)]
-        if depth > bands + EXTRA:
-            src.append(jnp.zeros((depth - bands - EXTRA, width), jnp.bfloat16))
-        src = jnp.concatenate(src, axis=0)
-        src_tall = src.T
+        own = slots[place]
+        src = deepened(own, bias_rows(None, width))
+        src_tall = deepened(own, bias_rows(lsw[place] + sp[place] - half_square(own), width)).T
         tiles = range(0, tgt_width, TILE)
         row_peak = None
         for at in tiles:
@@ -204,7 +213,7 @@
     every = row_stats[...]
     top = jnp.max(every[:, 0, :], axis=0, keepdims=True)
     total = jnp.sum(every[:, 1, :] * jnp.exp(every[:, 0, :] - top), axis=0, keepdims=True)
-    src_out[...] = 0.5 * (sp[me] + (lsw[me] + sp[me] - (top + jnp.log(total))))
+    src_out[...] = 0.5 * (sp[me] + (src_square - (top + jnp.log(total))))
 
     for k in range(1, copies):
         place = (rep + k) % copies

time: 16.8 us -> 16.7 us (level)
  no operation moved by 1% of the time
where the time goes in v5:
time: 16.7 us; the launch traced here: 16.6 us
  Pallas kernels  14.8 us (89%)
  local copies, waits for them, and re-layouts  1.16 us (7%)
  between operations  0.64 us (4%)
    pallas_call x1, Pallas kernels, on_device(): pl.pallas_call(functools.partial(kernel, blocks, copies), out_shape=(pltp...  14.8 us
    unnamed x2, local copies, waits for them, and re-layouts  1.16 us

profile of v5, /device:TPU:0, one launch (start us, length us, event | category | flops | bytes accessed | tf_op | source)
XLA Modules:
  0.0 16.6 jit_solution(8796538432667430868)
XLA Ops:
  0.6 14.8 %sinkhorn.1 = (f32[1,256]{1,0:T(1,128)S(1)}, f32[1,1024]{1,0:T(1,128)S(1)}) custom-call(bf16[64,256]{1,0:T(8,128)(2,1)} %src_hbm.1, bf16[64,1024]{1,0:T(8,128)(2,1)} %tgt_hbm.1, f32[1,256]{1,0:T(1,128)} %bitcast.10, f32[1,1024]{1,0:T(1,128)} %bitcast.8, f32[1,256]{1,0:T(1,128)} %bitcast.11, f32[1,1024]{1,0:T(1,128)} %bitcast.9), custom_call_target="tpu_custom_call" | custom-call | flops 268435456 | bytes 262144 | tf_op jit(solution)/shard_map/sinkhorn/pallas_call | solution.py:246
  15.4 0.6 %copy.10 = f32[256]{0:T(256)} copy(f32[256]{0:T(256)S(1)} %bitcast.7) | data formatting | bytes 2048
  16.0 0.6 %copy.11 = f32[1024]{0:T(1024)} copy(f32[1024]{0:T(1024)S(1)} %bitcast.6) | data formatting | bytes 8192

commit v6 on v5

--- a/solution.py
+++ b/solution.py
@@ -13,6 +13,7 @@
 EXTRA = 16
 DEPTH = 128
 TILE = 256
+LOG2_E = 1.4426950408889634
 
 
 def nearest(me, count, k):
@@ -22,6 +23,10 @@
     both = jnp.where(me * 2 < count, both, 2 * me - both)
     far = jnp.where(me * 2 < count, k, count - 1 - k)
     return jnp.where(k <= 2 * short, both, far)
+
+
+def power(value):
+    return jnp.exp2(value * LOG2_E)
 
 
 def in_three(value):
@@ -54,12 +59,12 @@
 
 def joined(earlier, later):
     peak = jnp.maximum(earlier[0], later[0])
-    return peak, earlier[1] * jnp.exp(earlier[0] - peak) + later[1] * jnp.exp(later[0] - peak)
+    return peak, earlier[1] * power(earlier[0] - peak) + later[1] * power(later[0] - peak)
 
 
 def folded(peak, total):
     top = jnp.max(peak, axis=0, keepdims=True)
-    return top, jnp.sum(total * jnp.exp(peak - top), axis=0, keepdims=True)
+    return top, jnp.sum(total * power(peak - top), axis=0, keepdims=True)
 
 
 def kernel(
@@ -177,7 +182,7 @@
         row_total = None
         for at in tiles:
             block = grouped(across[pl.ds(at, TILE), :], WIDE)
-            total = jnp.sum(jnp.exp(block - row_peak[None]), axis=0)
+            total = jnp.sum(power(block - row_peak[None]), axis=0)
             row_total = total if row_total is None else row_total + total
         top, total = folded(row_peak, row_total)
         stats = jnp.concatenate([top, total], axis=0)
@@ -193,7 +198,7 @@
 
         for at, peak in zip(tiles, col_peaks):
             here = (slice(None), pl.ds(at, TILE))
-            terms = jnp.exp(grouped(down[here], SUBLANES) - peak[None])
+            terms = power(grouped(down[here], SUBLANES) - peak[None])
             total = jnp.sum(terms.reshape(-1, WIDE, TILE), axis=0)
             total = jnp.sum(grouped(total, SUBLANES), axis=0)
             col_peak[here], col_total[here] = joined(
@@ -212,7 +217,7 @@
         row_copy(place, place).wait_recv()
     every = row_stats[...]
     top = jnp.max(every[:, 0, :], axis=0, keepdims=True)
-    total = jnp.sum(every[:, 1, :] * jnp.exp(every[:, 0, :] - top), axis=0, keepdims=True)
+    total = jnp.sum(every[:, 1, :] * power(every[:, 0, :] - top), axis=0, keepdims=True)
     src_out[...] = 0.5 * (sp[me] + (src_square - (top + jnp.log(total))))
 
     for k in range(1, copies):
@@ -220,7 +225,7 @@
         col_copy(place, place).wait_recv()
     every = col_stats[...]
     top = jnp.max(every[:, 0, :], axis=0, keepdims=True)
-    total = jnp.sum(every[:, 1, :] * jnp.exp(every[:, 0, :] - top), axis=0, keepdims=True)
+    total = jnp.sum(every[:, 1, :] * power(every[:, 0, :] - top), axis=0, keepdims=True)
     tgt_out[...] = 0.5 * (tp[...] + (tgt_bias - (top + jnp.log(total))))
 
     for k in range(1, blocks):

time: 16.7 us -> 16.7 us (level)
  no operation moved by 1% of the time
where the time goes in v6:
time: 16.7 us; the launch traced here: 16.6 us
  Pallas kernels  14.8 us (89%)
  local copies, waits for them, and re-layouts  1.16 us (7%)
  between operations  0.64 us (4%)
    pallas_call x1, Pallas kernels, on_device(): pl.pallas_call(functools.partial(kernel, blocks, copies), out_shape=(pltp...  14.8 us
    unnamed x2, local copies, waits for them, and re-layouts  1.16 us

profile of v6, /device:TPU:0, one launch (start us, length us, event | category | flops | bytes accessed | tf_op | source)
XLA Modules:
  0.0 16.6 jit_solution(6141227806038042227)
XLA Ops:
  0.6 14.8 %sinkhorn.1 = (f32[1,256]{1,0:T(1,128)S(1)}, f32[1,1024]{1,0:T(1,128)S(1)}) custom-call(bf16[64,256]{1,0:T(8,128)(2,1)} %src_hbm.1, bf16[64,1024]{1,0:T(8,128)(2,1)} %tgt_hbm.1, f32[1,256]{1,0:T(1,128)} %bitcast.10, f32[1,1024]{1,0:T(1,128)} %bitcast.8, f32[1,256]{1,0:T(1,128)} %bitcast.11, f32[1,1024]{1,0:T(1,128)} %bitcast.9), custom_call_target="tpu_custom_call" | custom-call | flops 268435456 | bytes 262144 | tf_op jit(solution)/shard_map/sinkhorn/pallas_call | solution.py:251
  15.4 0.6 %copy.10 = f32[256]{0:T(256)} copy(f32[256]{0:T(256)S(1)} %bitcast.7) | data formatting | bytes 2048
  16.0 0.6 %copy.11 = f32[1024]{0:T(1024)} copy(f32[1024]{0:T(1024)S(1)} %bitcast.6) | data formatting | bytes 8192
